TPU v7x, 32 devices: a whole 2x2x4 slice. The times are simulated.
32 devices in a mesh: group: 2 (over x), pos: 16 (over z, y, core).
Axes of the slice: x: 2, y: 2, z: 4, core: 2. Of those that a mesh axis runs over, the one named last changes fastest.
Arguments:
- acts: bfloat16 [4, 1024, 1536], P('group', 'pos'), parts along dimension 0, may hold values from -12 to 12
- skips: bfloat16 [4, 2048, 1280], P('group', 'pos'), parts along dimension 0, may hold values from -6 to 6
- norm_gain: float32 [1536], replicated, may hold values from 0.6 to 1.6
- w_query: bfloat16 [1536, 256], replicated, may hold values from -4 to 4
- w_key: bfloat16 [1536, 256], replicated, may hold values from -4 to 4
- w_value: bfloat16 [1536, 768], replicated, may hold values from -0.15625 to 0.15625
- w_out: bfloat16 [768, 1536], replicated, may hold values from -0.21875 to 0.21875
- w_lift: bfloat16 [1536, 1536], P('pos'), may hold values from -0.15625 to 0.15625
- w_skip: bfloat16 [1280, 1536], P('pos'), may hold values from -0.15625 to 0.15625
- depth_kernel: float32 [3, 1536], replicated, may hold values from -3 to 3
- w_point: bfloat16 [1536, 1536], P(None, 'pos'), may hold values from -0.15625 to 0.15625
Outputs:
- decoded: bfloat16 [4, 2048, 1536], P('group', 'pos'), parts along dimension 0
There are 2 independent parts, one for each index of `group`. A program takes and returns all parts, laid end to end along the dimension named above; an argument that names none is the same for every part. Nothing has to cross between parts.
All inputs are finite; a program needn't handle non-finite values.
Results may differ from a plain program's by a relative error of at most 0.014.
Values may be sent and summed in bfloat16 or wider, within the bound.
A program may use at most 128 MiB of HBM per device.

v0:
```python
import jax
import jax.numpy as jnp
from jax import lax
from jax.sharding import PartitionSpec as P

HEADS = 4
HK = 64
HV = 192


def extended(cells, sides, width):
    for axis, dim in sides:
        count = lax.axis_size(axis)
        ends = count - 1
        head = lax.slice_in_dim(cells, 0, width, axis=dim)
        tail = lax.slice_in_dim(cells, cells.shape[dim] - width, cells.shape[dim], axis=dim)
        cells = jnp.concatenate(
            [
                lax.ppermute(tail, axis, [(i, (i + 1) % count) for i in range(ends)]),
                cells,
                lax.ppermute(head, axis, [((i + 1) % count, i) for i in range(ends)]),
            ],
            axis=dim,
        )
    return cells


def on_device(
    acts, skips, norm_gain, w_query, w_key, w_value, w_out, w_lift, w_skip, depth_kernel, w_point
):
    lift_full, skip_full, point_full = (
        lax.all_gather(w_lift, "pos", axis=0, tiled=True),
        lax.all_gather(w_skip, "pos", axis=0, tiled=True),
        lax.all_gather(w_point, "pos", axis=1, tiled=True),
    )
    seq_count, bin_rows, width = acts.shape
    actsf = acts.astype(jnp.float32)
    centre = actsf - jnp.mean(actsf, axis=-1, keepdims=True)
    normed = (
        centre * lax.rsqrt(jnp.mean(centre * centre, axis=-1, keepdims=True) + 1e-05) * norm_gain
    ).astype(jnp.bfloat16)
    flat = normed.reshape(seq_count * bin_rows, width)
    queries = (
        (jnp.dot(flat, w_query, preferred_element_type=jnp.float32) * HK ** (-0.5))
        .astype(jnp.bfloat16)
        .reshape(seq_count, bin_rows, HEADS, HK)
    )
    keys_here = (
        jnp.dot(flat, w_key, preferred_element_type=jnp.float32)
        .astype(jnp.bfloat16)
        .reshape(seq_count, bin_rows, HEADS * HK)
    )
    values_here = (
        jnp.dot(flat, w_value, preferred_element_type=jnp.float32)
        .astype(jnp.bfloat16)
        .reshape(seq_count, bin_rows, HEADS * HV)
    )
    running = jnp.full((seq_count, HEADS, bin_rows), -1e30, jnp.float32)
    key_piece = lax.all_gather(keys_here, "pos", axis=1, tiled=True)
    value_piece = lax.all_gather(values_here, "pos", axis=1, tiled=True)
    count = key_piece.shape[1]
    keyed = key_piece.reshape(seq_count, count, HEADS, HK)
    valued = value_piece.reshape(seq_count, count, HEADS, HV)
    scores = jnp.einsum("sqhd,skhd->shqk", queries, keyed, preferred_element_type=jnp.float32)
    newest = jnp.maximum(running, jnp.max(scores, axis=-1))
    weights = jnp.exp(scores - newest[..., None])
    totals = jnp.sum(weights, axis=-1)
    summed = jnp.einsum(
        "shqk,skhv->shqv", weights.astype(jnp.bfloat16), valued, preferred_element_type=jnp.float32
    )
    running, totals, summed = (newest, totals, summed)
    mixed = (
        (summed / totals[..., None])
        .transpose(0, 2, 1, 3)
        .reshape(seq_count * bin_rows, HEADS * HV)
        .astype(jnp.bfloat16)
    )
    attended = (
        actsf.reshape(seq_count * bin_rows, width)
        + jnp.dot(mixed, w_out, preferred_element_type=jnp.float32)
    ).astype(jnp.bfloat16)
    activated = jax.nn.gelu(attended.astype(jnp.float32)).astype(jnp.bfloat16)
    lifted = jnp.dot(activated, lift_full, preferred_element_type=jnp.float32)
    lifted = lifted.astype(jnp.bfloat16).reshape(seq_count, bin_rows, width)
    raised = jnp.repeat(lifted, 2, axis=1).reshape(seq_count * 2 * bin_rows, width)
    skip_act = (
        jax.nn.gelu(skips.astype(jnp.float32))
        .astype(jnp.bfloat16)
        .reshape(seq_count * 2 * bin_rows, skips.shape[2])
    )
    skip_term = jnp.dot(skip_act, skip_full, preferred_element_type=jnp.float32)
    merged = (
        (raised.astype(jnp.float32) + skip_term)
        .astype(jnp.bfloat16)
        .reshape(seq_count, 2 * bin_rows, width)
    )
    padded = extended(merged, (("pos", 1),), 1)
    paddedf = padded.astype(jnp.float32)
    spread = (
        depth_kernel[0] * paddedf[:, :-2]
        + depth_kernel[1] * paddedf[:, 1:-1]
        + depth_kernel[2] * paddedf[:, 2:]
    ).astype(jnp.bfloat16)
    spread = spread.reshape(seq_count * 2 * bin_rows, width)
    decoded = jnp.dot(spread, point_full, preferred_element_type=jnp.float32)
    return decoded.astype(jnp.bfloat16).reshape(seq_count, 2 * bin_rows, width)


def solution(mesh):
    return jax.shard_map(
        on_device,
        mesh=mesh,
        in_specs=(
            P("group", "pos", None),
            P("group", "pos", None),
            P(),
            P(),
            P(),
            P(),
            P(),
            P("pos", None),
            P("pos", None),
            P(),
            P(None, "pos"),
        ),
        out_specs=P("group", "pos", None),
        check_vma=False,
    )
```

profile of v0, /device:TPU:0, one launch (start us, length us, event | category | flops | bytes accessed | tf_op | source)
XLA Modules:
  0.0 268.4 jit_solution(8063212985456525454)
XLA Ops:
  6.5 1.3 convert_reduce_fusion
  7.8 1.3 multiply_reduce_fusion
  9.1 1.3 multiply_convert_fusion
  10.4 0.9 convolution_convert_fusion.3
  11.4 2.9 %convolution_convert_fusion.2 = bf16[128,768]{1,0:T(8,128)(2,1)} fusion(bf16[128,1536]{1,0:T(8,128)(2,1)S(1)} %bitcast.36, bf16[1536,768]{1,0:T(8,128)(2,1)} %param.16), kind=kOutput, calls=%fused_computation.30 | convolution fusion | flops 302088192 | bytes 2949120 | tf_op jit(solution)/shard_map/dot_general | solution.py:54
  14.3 0.7 all-gather.10.cloned.1.call-update
  15.1 0.5 all-gather.12.cloned.1.call-update
  15.6 0.5 all-gather.14.cloned.1.call-update
  16.2 0.9 fusion.16
  17.1 1.0 reshape.61
  18.1 2.4 fusion.13
  20.4 31.7 %all-gather.6.cloned.1.call-done = bf16[2,1024,256]{2,1,0:T(8,128)(2,1)} async-done(((bf16[2,64,256]{2,1,0:T(8,128)(2,1)}), bf16[2,1024,256]{2,1,0:T(8,128)(2,1)}) %all-gather.6.cloned.1.call-update) | async-done | bytes 1048592 | tf_op jit(solution)/shard_map/all_gather | solution.py:59
  52.1 1.5 copy.15
  53.6 0.5 fusion.38
  54.1 1.3 copy-done.1
  55.5 0.5 fusion.3
  56.0 42.6 %all-gather.8.cloned.1.call-done = bf16[2,1024,768]{2,1,0:T(8,128)(2,1)} async-done(((bf16[2,64,768]{2,1,0:T(8,128)(2,1)}), bf16[2,1024,768]{2,1,0:T(8,128)(2,1)}) %all-gather.8.cloned.1.call-update) | async-done | bytes 3145744 | tf_op jit(solution)/shard_map/all_gather | solution.py:60
  98.6 4.6 %copy.17 = bf16[2,1024,768]{1,2,0:T(8,128)(2,1)} copy(bf16[2,1024,768]{2,1,0:T(8,128)(2,1)} %all-gather.8.cloned.1.call-done) | data formatting | bytes 6291456 | tf_op jit(solution)/shard_map/all_gather | solution.py:60
  103.2 3.7 %fusion.15 = bf16[2,64,4,192]{3,1,2,0:T(8,128)(2,1)S(1)} fusion(bf16[2,1024,4,192]{1,3,2,0:T(8,128)(2,1)} %bitcast.40, f32[2,4,64,1024]{3,2,1,0:T(8,128)} %copy-done.1, f32[2,4,64]{2,1,0:T(4,128)S(1)} %broadcast_maximum_fusion, f32[2,64,4]{1,2,0:T(4,128)S(1)} %bitcast.48), kind=kOutput, calls=%fused_computation.28 | convolution fusion | flops 202571776 | bytes 5443584 | tf_op jit(solution)/shard_map/shqk,skhv->shqv/dot_general | solution.py:68
  107.4 45.7 %all-gather.10.cloned.1.call-done = bf16[1536,1536]{1,0:T(8,128)(2,1)} async-done(((bf16[96,1536]{1,0:T(8,128)(2,1)}), bf16[1536,1536]{1,0:T(8,128)(2,1)}) %all-gather.10.cloned.1.call-update) | async-done | bytes 4718608 | tf_op jit(solution)/shard_map/all_gather | solution.py:32
  153.1 3.7 %convolution_convert_fusion.1 = bf16[128,1536]{1,0:T(8,128)(2,1)S(1)} fusion(bf16[1536,1536]{1,0:T(8,128)(2,1)} %all-gather.10.cloned.1.call-done, bf16[128,768]{1,0:T(8,128)(2,1)S(1)} %convert_element_type.71, bf16[768,1536]{1,0:T(8,128)(2,1)S(1)} %copy-done, bf16[128,1536]{1,0:T(8,128)(2,1)S(1)} %bitcast.39), kind=kOutput, calls=%fused_computation.6 | convolution fusion | flops 908722176 | bytes 8060928 | tf_op jit(solution)/shard_map/dot_general | solution.py:83
  156.8 1.6 broadcast_in_dim.5
  158.3 3.2 %convert_element_type.78 = f32[256,1536]{1,0:T(8,128)} reshape(f32[2,64,2,1536]{3,2,1,0:T(2,128)} %broadcast_in_dim.5) | data formatting | bytes 3145728 | tf_op jit(solution)/shard_map/convert_element_type | solution.py:93
  161.5 41.0 %all-gather.12.cloned.1.call-done = bf16[1280,1536]{1,0:T(8,128)(2,1)} async-done(((bf16[80,1536]{1,0:T(8,128)(2,1)}), bf16[1280,1536]{1,0:T(8,128)(2,1)}) %all-gather.12.cloned.1.call-update) | async-done | bytes 3932176 | tf_op jit(solution)/shard_map/all_gather | solution.py:33
  202.6 3.8 %fusion = bf16[256,1536]{1,0:T(8,128)(2,1)S(1)} fusion(f32[256,1536]{1,0:T(8,128)} %convert_element_type.78, bf16[256,1280]{1,0:T(8,128)(2,1)S(1)} %bitcast.45, bf16[1280,1536]{1,0:T(8,128)(2,1)} %all-gather.12.cloned.1.call-done), kind=kOutput, calls=%fused_computation.1 | convolution fusion | flops 1007419392 | bytes 6946816 | tf_op jit(solution)/shard_map/dot_general | solution.py:91
  206.4 2.2 collective-permute-start
  208.6 1.3 collective-permute-start.1
  210.0 1.7 collective-permute-done.1
  211.7 0.2 maximum_convert_fusion
  211.9 0.5 fusion.6
  212.4 44.8 %all-gather.14.cloned.1.call-done = bf16[1536,1536]{0,1:T(8,128)(2,1)} async-done(((bf16[1536,96]{0,1:T(8,128)(2,1)}), bf16[1536,1536]{0,1:T(8,128)(2,1)}) %all-gather.14.cloned.1.call-update) | async-done | bytes 4718608 | tf_op jit(solution)/shard_map/all_gather | solution.py:34
  257.2 4.6 %convolution_convert_fusion = bf16[256,1536]{1,0:T(8,128)(2,1)} fusion(bf16[256,1536]{1,0:T(8,128)(2,1)S(1)} %bitcast.44, bf16[1536,1536]{0,1:T(8,128)(2,1)} %all-gather.14.cloned.1.call-done), kind=kOutput, calls=%fused_computation.2 | convolution fusion | flops 1208352768 | bytes 6291456 | tf_op jit(solution)/shard_map/dot_general | solution.py:105
  (28 shorter events, 0.8 us)
Async XLA Ops:
  6.5 146.6 %copy-start = (bf16[768,1536]{1,0:T(8,128)(2,1)S(1)}, bf16[768,1536]{1,0:T(8,128)(2,1)}, u32[]{:S(2)}) copy-start(bf16[768,1536]{1,0:T(8,128)(2,1)} %param.17) | copy-start | bytes 7077892
  6.5 3.8 %copy-start.3 = (bf16[1536,256]{1,0:T(8,128)(2,1)S(1)}, bf16[1536,256]{1,0:T(8,128)(2,1)}, u32[]{:S(2)}) copy-start(bf16[1536,256]{1,0:T(8,128)(2,1)} %param.15) | copy-start | bytes 2359300
  6.5 45.6 %all-gather.6.cloned.1.call-start = ((), (), s32[]{:S(2)}) async-start(), calls=%async_computation | async-start | bytes 1114112 | tf_op jit(solution)/shard_map/all_gather | solution.py:59
  11.3 4.9 %copy-start.4 = (bf16[1536,256]{1,0:T(8,128)(2,1)S(1)}, bf16[1536,256]{1,0:T(8,128)(2,1)}, u32[]{:S(2)}) copy-start(bf16[1536,256]{1,0:T(8,128)(2,1)} %param.14) | copy-start | bytes 2359300
  11.3 87.3 %all-gather.8.cloned.1.call-start = ((), (), s32[]{:S(2)}) async-start(), calls=%async_computation.1 | async-start | bytes 3342336 | tf_op jit(solution)/shard_map/all_gather | solution.py:60
  14.3 138.8 %all-gather.10.cloned.1.call-start = ((), (), s32[]{:S(2)}) async-start(), calls=%async_computation.2 | async-start | bytes 5013504 | tf_op jit(solution)/shard_map/all_gather | solution.py:32
  15.0 187.6 %all-gather.12.cloned.1.call-start = ((), (), s32[]{:S(2)}) async-start(), calls=%async_computation.3 | async-start | bytes 4177920 | tf_op jit(solution)/shard_map/all_gather | solution.py:33
  15.6 241.7 %all-gather.14.cloned.1.call-start = ((), (), s32[]{:S(2)}) async-start(), calls=%async_computation.4 | async-start | bytes 5013504 | tf_op jit(solution)/shard_map/all_gather | solution.py:34
  54.1 1.4 copy-start.1
  103.2 49.9 %copy-start.2 = (bf16[2,64,1536]{2,1,0:T(8,128)(2,1)S(1)}, bf16[2,64,1536]{2,1,0:T(8,128)(2,1)}, u32[]{:S(2)}) copy-start(bf16[2,64,1536]{2,1,0:T(8,128)(2,1)} %param.11) | copy-start | bytes 1179652
  158.3 44.3 %copy-start.5 = (bf16[2,128,1280]{2,1,0:T(8,128)(2,1)S(1)}, bf16[2,128,1280]{2,1,0:T(8,128)(2,1)}, u32[]{:S(2)}) copy-start(bf16[2,128,1280]{2,1,0:T(8,128)(2,1)} %fusion.13) | copy-start | bytes 1966084
  202.6 7.3 %copy-start.6 = (f32[3,1536]{1,0:T(4,128)S(1)}, f32[3,1536]{1,0:T(4,128)}, u32[]{:S(2)}) copy-start(f32[3,1536]{1,0:T(4,128)} %param.20) | copy-start | bytes 55300
  206.4 3.5 %collective-permute-start = (bf16[2,1,1536]{2,1,0:T(2,128)(2,1)S(1)}, bf16[2,1,1536]{2,1,0:T(2,128)(2,1)S(1)}, u32[]{:S(2)}, u32[]{:S(2)}) collective-permute-start(bf16[2,1,1536]{2,1,0:T(2,128)(2,1)S(1)} %get-tuple-element.8), channel_id=1, source_target_pairs={{0,1},{1,2},{2,3},{3,4},{4,5},{5,6},{6,7},{7,8},{8,9},{9,10},{10,1... | collective-permute-start | bytes 18440 | tf_op jit(solution)/shard_map/ppermute | solution.py:19
  208.6 3.1 %collective-permute-start.1 = (bf16[2,1,1536]{2,1,0:T(2,128)(2,1)S(1)}, bf16[2,1,1536]{2,1,0:T(2,128)(2,1)S(1)}, u32[]{:S(2)}, u32[]{:S(2)}) collective-permute-start(bf16[2,1,1536]{2,1,0:T(2,128)(2,1)S(1)} %get-tuple-element.9), channel_id=1, source_target_pairs={{1,0},{2,1},{3,2},{4,3},{5,4},{6,5},{7,6},{8,7},{9,8},{10,9},{11,1... | collective-permute-start | bytes 18440 | tf_op jit(solution)/shard_map/ppermute | solution.py:21
Sparse Core Ops, SparseCore 0:
  11.4 40.6 all-gather.5
  54.4 44.1 all-gather.7
  100.9 52.1 all-gather.9
  155.2 47.3 all-gather.11
  204.7 52.4 all-gather.13
where the time goes:
time: 269 us; the launch traced here: 268 us
  waiting for transfers between devices  209 us (78%)
  matrix products  21 us (8%)
  local copies, waits for them, and re-layouts  13.7 us (5%)
  between operations  13.3 us (5%)
  other arithmetic  7.44 us (3%)
  starting transfers between devices  3.61 us (1%)
    all_gather x1, waiting for transfers between devices, on_device(): lax.all_gather(w_lift, 'pos', axis=0, tiled=True)  45.7 us
    all_gather x1, waiting for transfers between devices, on_device(): lax.all_gather(w_point, 'pos', axis=1, tiled=True)  44.8 us
    all_gather x1, waiting for transfers between devices, on_device(): value_piece = lax.all_gather(values_here, 'pos', axis=1, tiled=True)  42.6 us
    all_gather x1, waiting for transfers between devices, on_device(): lax.all_gather(w_skip, 'pos', axis=0, tiled=True)  41 us
    all_gather x1, waiting for transfers between devices, on_device(): key_piece = lax.all_gather(keys_here, 'pos', axis=1, tiled=True)  31.7 us
  transfers between devices with their start and end apart: 7, of which 6 were waited for; matrix products, arithmetic and copies ran while one was open for 12% of the time, Pallas kernels for 0%

commit v1 on v0

--- a/solution.py
+++ b/solution.py
@@ -56,7 +56,25 @@
         .reshape(seq_count, bin_rows, HEADS * HV)
     )
     running = jnp.full((seq_count, HEADS, bin_rows), -1e30, jnp.float32)
-    key_piece = lax.all_gather(keys_here, "pos", axis=1, tiled=True)
+    devices, index, rows = (lax.axis_size("pos"), lax.axis_index("pos"), keys_here.shape[1])
+    right = [(i_2, (i_2 + 1) % devices) for i_2 in range(devices)]
+    behind = [(i_2, (i_2 - 1) % devices) for i_2 in range(devices)]
+    key_piece = jnp.zeros(
+        (*keys_here.shape[:1], devices * rows, *keys_here.shape[1 + 1 :]), keys_here.dtype
+    )
+    key_piece = lax.dynamic_update_slice_in_dim(key_piece, keys_here, index * rows, axis=1)
+    from_left = from_right = keys_here
+    middle = devices // 2
+    for step in range(1, middle + 1):
+        from_left = lax.ppermute(from_left, "pos", right)
+        key_piece = lax.dynamic_update_slice_in_dim(
+            key_piece, from_left, (index - step) % devices * rows, axis=1
+        )
+        if step < devices - middle:
+            from_right = lax.ppermute(from_right, "pos", behind)
+            key_piece = lax.dynamic_update_slice_in_dim(
+                key_piece, from_right, (index + step) % devices * rows, axis=1
+            )
     value_piece = lax.all_gather(values_here, "pos", axis=1, tiled=True)
     count = key_piece.shape[1]
     keyed = key_piece.reshape(seq_count, count, HEADS, HK)

time: 269 us -> 236 us (0.88)
  waiting for transfers between devices: 209 us -> 96.6 us
  local copies, waits for them, and re-layouts: 13.7 us -> 60.5 us
  starting transfers between devices: 3.61 us -> 37.1 us
    all_gather x1, waiting for transfers between devices: 45.7 us -> 0.02 us  [on_device(): lax.all_gather(w_lift, 'pos', axis=0, tiled=True)]
    all_gather x1, waiting for transfers between devices: 42.6 us -> 0.02 us  [on_device(): value_piece = lax.all_gather(values_here, 'pos', axis=1, tiled=True)]
    ppermute x0 -> x15, starting transfers between devices: none -> 33.5 us  [the longest x7 33 us: on_device(): from_right = lax.ppermute(from_right, 'pos', behind)]
    all_gather x1 -> x0, waiting for transfers between devices: 31.7 us -> none  [on_device(): key_piece = lax.all_gather(keys_here, 'pos', axis=1, tiled=True)]
    dynamic_update_slice x0 -> x16, local copies, waits for them, and re-layouts: none -> 24.1 us  [the longest x8 11.9 us: on_device(): lax.dynamic_update_slice_in_dim(key_piece, from_left, (index - step) % de...]
    ppermute x0 -> x15, local copies, waits for them, and re-layouts: none -> 23.8 us  [the longest x8 12.7 us: on_device(): from_left = lax.ppermute(from_left, 'pos', right)]
    ppermute x0 -> x15, waiting for transfers between devices: none -> 12.9 us  [the longest x8 7.46 us: on_device(): from_left = lax.ppermute(from_left, 'pos', right)]
    all_gather x1, waiting for transfers between devices: 41 us -> 35.2 us  [on_device(): lax.all_gather(w_skip, 'pos', axis=0, tiled=True)]
  transfers between devices with their start and end apart: 7 -> 21, of which waited for: 6 -> 15; matrix products, arithmetic and copies ran while one was open for 12% -> 32% of each run, Pallas kernels for 0% -> 0%
where the time goes in v1:
time: 236 us; the launch traced here: 235 us
  waiting for transfers between devices  96.6 us (41%)
  local copies, waits for them, and re-layouts  60.5 us (26%)
  starting transfers between devices  37.1 us (16%)
  matrix products  19.8 us (8%)
  between operations  13.7 us (6%)
  other arithmetic  7.46 us (3%)
    all_gather x1, waiting for transfers between devices, on_device(): lax.all_gather(w_point, 'pos', axis=1, tiled=True)  44.9 us
    all_gather x1, waiting for transfers between devices, on_device(): lax.all_gather(w_skip, 'pos', axis=0, tiled=True)  35.2 us
    ppermute x7, starting transfers between devices, on_device(): from_right = lax.ppermute(from_right, 'pos', behind)  33 us
    ppermute x8, local copies, waits for them, and re-layouts, on_device(): from_left = lax.ppermute(from_left, 'pos', right)  12.7 us
    dynamic_update_slice x8, local copies, waits for them, and re-layouts, on_device(): lax.dynamic_update_slice_in_dim(key_piece, from_left, (index - step) % de...  11.9 us
    ppermute x7, local copies, waits for them, and re-layouts, on_device(): from_right = lax.ppermute(from_right, 'pos', behind)  11.1 us
    dynamic_update_slice x7, local copies, waits for them, and re-layouts, on_device(): lax.dynamic_update_slice_in_dim(key_piece, from_right, (index + step) % d...  10.8 us
    ppermute x8, waiting for transfers between devices, on_device(): from_left = lax.ppermute(from_left, 'pos', right)  7.46 us
  transfers between devices with their start and end apart: 21, of which 15 were waited for; matrix products, arithmetic and copies ran while one was open for 32% of the time, Pallas kernels for 0%

profile of v1, /device:TPU:0, one launch (start us, length us, event | category | flops | bytes accessed | tf_op | source)
XLA Modules:
  0.0 235.1 jit_solution(16190436364745730499)
XLA Ops:
  10.4 2.9 %convolution_convert_fusion.2 = bf16[128,768]{1,0:T(8,128)(2,1)} fusion(bf16[128,1536]{1,0:T(8,128)(2,1)S(1)} %bitcast.35, bf16[1536,768]{1,0:T(8,128)(2,1)} %param.16), kind=kOutput, calls=%fused_computation.30 | convolution fusion | flops 302088192 | bytes 2949120 | tf_op jit(solution)/shard_map/dot_general | solution.py:54
  16.3 5.4 %collective-permute-start.1 = (bf16[2,64,256]{2,1,0:T(8,128)(2,1)S(1)}, bf16[2,64,256]{2,1,0:T(8,128)(2,1)S(1)}, u32[]{:S(2)}, u32[]{:S(2)}) collective-permute-start(bf16[2,64,256]{2,1,0:T(8,128)(2,1)S(1)} %bitcast.48), channel_id=1, source_target_pairs={{0,15},{1,0},{2,1},{3,2},{4,3},{5,4},{6,5},{7,6},{8,7},{9,8},{10,9... | collective-permute-start | bytes 196616 | tf_op jit(solution)/shard_map/ppermute | solution.py:74
  23.6 4.5 %collective-permute-start.3 = (bf16[2,64,256]{2,1,0:T(8,128)(2,1)S(1)}, bf16[2,64,256]{2,1,0:T(8,128)(2,1)S(1)}, u32[]{:S(2)}, u32[]{:S(2)}) collective-permute-start(bf16[2,64,256]{2,1,0:T(8,128)(2,1)S(1)} %collective-permute-done.1), channel_id=1, source_target_pairs={{0,15},{1,0},{2,1},{3,2},{4,3},{5,4},{6,5},{7,6},{8,7},{9,8},{10,9... | collective-permute-start | bytes 196616 | tf_op jit(solution)/shard_map/ppermute | solution.py:74
  28.1 1.7 collective-permute-done.2
  31.0 4.7 %collective-permute-start.5 = (bf16[2,64,256]{2,1,0:T(8,128)(2,1)S(1)}, bf16[2,64,256]{2,1,0:T(8,128)(2,1)S(1)}, u32[]{:S(2)}, u32[]{:S(2)}) collective-permute-start(bf16[2,64,256]{2,1,0:T(8,128)(2,1)S(1)} %collective-permute-done.3), channel_id=1, source_target_pairs={{0,15},{1,0},{2,1},{3,2},{4,3},{5,4},{6,5},{7,6},{8,7},{9,8},{10,9... | collective-permute-start | bytes 196616 | tf_op jit(solution)/shard_map/ppermute | solution.py:74
  37.6 4.5 %collective-permute-start.7 = (bf16[2,64,256]{2,1,0:T(8,128)(2,1)S(1)}, bf16[2,64,256]{2,1,0:T(8,128)(2,1)S(1)}, u32[]{:S(2)}, u32[]{:S(2)}) collective-permute-start(bf16[2,64,256]{2,1,0:T(8,128)(2,1)S(1)} %collective-permute-done.5), channel_id=1, source_target_pairs={{0,15},{1,0},{2,1},{3,2},{4,3},{5,4},{6,5},{7,6},{8,7},{9,8},{10,9... | collective-permute-start | bytes 196616 | tf_op jit(solution)/shard_map/ppermute | solution.py:74
  43.2 1.8 collective-permute-done.7
  45.0 4.7 %collective-permute-start.9 = (bf16[2,64,256]{2,1,0:T(8,128)(2,1)S(1)}, bf16[2,64,256]{2,1,0:T(8,128)(2,1)S(1)}, u32[]{:S(2)}, u32[]{:S(2)}) collective-permute-start(bf16[2,64,256]{2,1,0:T(8,128)(2,1)S(1)} %collective-permute-done.7), channel_id=1, source_target_pairs={{0,15},{1,0},{2,1},{3,2},{4,3},{5,4},{6,5},{7,6},{8,7},{9,8},{10,9... | collective-permute-start | bytes 196616 | tf_op jit(solution)/shard_map/ppermute | solution.py:74
  51.9 4.8 %collective-permute-start.11 = (bf16[2,64,256]{2,1,0:T(8,128)(2,1)S(1)}, bf16[2,64,256]{2,1,0:T(8,128)(2,1)}, u32[]{:S(2)}, u32[]{:S(2)}) collective-permute-start(bf16[2,64,256]{2,1,0:T(8,128)(2,1)S(1)} %collective-permute-done.9), channel_id=1, source_target_pairs={{0,15},{1,0},{2,1},{3,2},{4,3},{5,4},{6,5},{7,6},{8,7},{9,8},{10,9... | collective-permute-start | bytes 196616 | tf_op jit(solution)/shard_map/ppermute | solution.py:74
  57.5 2.4 %fusion.13 = bf16[2,128,1280]{2,1,0:T(8,128)(2,1)} fusion(bf16[2,128,1280]{2,1,0:T(8,128)(2,1)} %param.12), kind=kLoop, calls=%fused_computation.25 | loop fusion | flops 3276800 | bytes 1310720 | tf_op jit(solution)/shard_map/convert_element_type | solution.py:106
  59.9 4.4 %collective-permute-start.13 = (bf16[2,64,256]{2,1,0:T(8,128)(2,1)}, bf16[2,64,256]{2,1,0:T(8,128)(2,1)}, u32[]{:S(2)}, u32[]{:S(2)}) collective-permute-start(bf16[2,64,256]{2,1,0:T(8,128)(2,1)} %collective-permute-done.11), channel_id=1, source_target_pairs={{0,15},{1,0},{2,1},{3,2},{4,3},{5,4},{6,5},{7,6},{8,7},{9,8},{10,9... | collective-permute-start | bytes 196616 | tf_op jit(solution)/shard_map/ppermute | solution.py:74
  69.1 1.7 dynamic_update_slice.49
  72.4 1.8 dynamic_update_slice.50
  74.2 1.6 copy.33
  79.8 1.6 copy.35
  81.4 1.8 dynamic_update_slice.53
  83.1 1.6 copy.36
  84.7 1.8 dynamic_update_slice.54
  93.7 1.8 dynamic_update_slice.57
  97.1 1.8 dynamic_update_slice.58
  106.1 1.8 dynamic_update_slice.61
  109.5 1.8 dynamic_update_slice.62
  116.5 4.7 %copy.47 = bf16[2,1024,768]{1,2,0:T(8,128)(2,1)} copy(bf16[2,1024,768]{2,1,0:T(8,128)(2,1)} %all-gather.5.cloned.1.call-done) | data formatting | bytes 6291456 | tf_op jit(solution)/shard_map/all_gather | solution.py:78
  121.3 3.7 %fusion.15 = bf16[2,64,4,192]{3,1,2,0:T(8,128)(2,1)S(1)} fusion(bf16[2,1024,4,192]{1,3,2,0:T(8,128)(2,1)} %bitcast.40, f32[2,4,64,1024]{3,2,1,0:T(8,128)} %copy-done.1, f32[2,4,64]{2,1,0:T(4,128)S(1)} %broadcast_maximum_fusion, f32[2,64,4]{1,2,0:T(4,128)S(1)} %bitcast.50), kind=kOutput, calls=%fused_computation.28 | convolution fusion | flops 202571776 | bytes 5443584 | tf_op jit(solution)/shard_map/shqk,skhv->shqv/dot_general | solution.py:86
  125.5 3.7 %convolution_convert_fusion.1 = bf16[128,1536]{1,0:T(8,128)(2,1)S(1)} fusion(bf16[1536,1536]{1,0:T(8,128)(2,1)} %all-gather.7.cloned.1.call-done, bf16[128,768]{1,0:T(8,128)(2,1)S(1)} %convert_element_type.71, bf16[768,1536]{1,0:T(8,128)(2,1)S(1)} %copy-done, bf16[128,1536]{1,0:T(8,128)(2,1)S(1)} %bitcast.39), kind=kOutput, calls=%fused_computation.6 | convolution fusion | flops 908722176 | bytes 8060928 | tf_op jit(solution)/shard_map/dot_general | solution.py:101
  130.8 3.3 %convert_element_type.78 = f32[256,1536]{1,0:T(8,128)} reshape(f32[2,64,2,1536]{3,2,1,0:T(2,128)} %broadcast_in_dim.16) | data formatting | bytes 3145728 | tf_op jit(solution)/shard_map/convert_element_type | solution.py:111
  134.0 35.2 %all-gather.9.cloned.1.call-done = bf16[1280,1536]{1,0:T(8,128)(2,1)} async-done(((bf16[80,1536]{1,0:T(8,128)(2,1)}), bf16[1280,1536]{1,0:T(8,128)(2,1)}) %all-gather.9.cloned.1.call-update) | async-done | bytes 3932176 | tf_op jit(solution)/shard_map/all_gather | solution.py:33
  169.3 3.8 %fusion = bf16[256,1536]{1,0:T(8,128)(2,1)S(1)} fusion(f32[256,1536]{1,0:T(8,128)} %convert_element_type.78, bf16[256,1280]{1,0:T(8,128)(2,1)S(1)} %bitcast.45, bf16[1280,1536]{1,0:T(8,128)(2,1)} %all-gather.9.cloned.1.call-done), kind=kOutput, calls=%fused_computation.1 | convolution fusion | flops 1007419392 | bytes 6946816 | tf_op jit(solution)/shard_map/dot_general | solution.py:109
  173.1 2.2 collective-permute-start.15
  176.6 1.7 collective-permute-done.16
  179.1 44.9 %all-gather.11.cloned.1.call-done = bf16[1536,1536]{0,1:T(8,128)(2,1)} async-done(((bf16[1536,96]{0,1:T(8,128)(2,1)}), bf16[1536,1536]{0,1:T(8,128)(2,1)}) %all-gather.11.cloned.1.call-update) | async-done | bytes 4718608 | tf_op jit(solution)/shard_map/all_gather | solution.py:34
  223.9 4.6 %convolution_convert_fusion = bf16[256,1536]{1,0:T(8,128)(2,1)} fusion(bf16[256,1536]{1,0:T(8,128)(2,1)S(1)} %bitcast.44, bf16[1536,1536]{0,1:T(8,128)(2,1)} %all-gather.11.cloned.1.call-done), kind=kOutput, calls=%fused_computation.2 | convolution fusion | flops 1208352768 | bytes 6291456 | tf_op jit(solution)/shard_map/dot_general | solution.py:123
  (113 shorter events, 52.9 us)
Async XLA Ops:
  6.5 118.9 %copy-start = (bf16[768,1536]{1,0:T(8,128)(2,1)S(1)}, bf16[768,1536]{1,0:T(8,128)(2,1)}, u32[]{:S(2)}) copy-start(bf16[768,1536]{1,0:T(8,128)(2,1)} %param.17) | copy-start | bytes 7077892
  6.5 110.0 %all-gather.5.cloned.1.call-start = ((), (), s32[]{:S(2)}) async-start(), calls=%async_computation | async-start | bytes 3342336 | tf_op jit(solution)/shard_map/all_gather | solution.py:78
  13.3 112.2 %all-gather.7.cloned.1.call-start = ((), (), s32[]{:S(2)}) async-start(), calls=%async_computation.1 | async-start | bytes 5013504 | tf_op jit(solution)/shard_map/all_gather | solution.py:32
  14.1 155.2 %all-gather.9.cloned.1.call-start = ((), (), s32[]{:S(2)}) async-start(), calls=%async_computation.2 | async-start | bytes 4177920 | tf_op jit(solution)/shard_map/all_gather | solution.py:33
  14.8 209.1 %all-gather.11.cloned.1.call-start = ((), (), s32[]{:S(2)}) async-start(), calls=%async_computation.3 | async-start | bytes 5013504 | tf_op jit(solution)/shard_map/all_gather | solution.py:34
  15.4 49.2 %copy-start.4 = (bf16[1536,256]{1,0:T(8,128)(2,1)S(1)}, bf16[1536,256]{1,0:T(8,128)(2,1)}, u32[]{:S(2)}) copy-start(bf16[1536,256]{1,0:T(8,128)(2,1)} %param.14) | copy-start | bytes 2359300
  15.7 7.6 %collective-permute-start = (bf16[2,64,256]{2,1,0:T(8,128)(2,1)S(1)}, bf16[2,64,256]{2,1,0:T(8,128)(2,1)S(1)}, u32[]{:S(2)}, u32[]{:S(2)}) collective-permute-start(bf16[2,64,256]{2,1,0:T(8,128)(2,1)S(1)} %bitcast.47), channel_id=1, source_target_pairs={{0,1},{1,2},{2,3},{3,4},{4,5},{5,6},{6,7},{7,8},{8,9},{9,10},{10,1... | collective-permute-start | bytes 196616 | tf_op jit(solution)/shard_map/ppermute | solution.py:69
  16.3 7.4 %collective-permute-start.1 = (bf16[2,64,256]{2,1,0:T(8,128)(2,1)S(1)}, bf16[2,64,256]{2,1,0:T(8,128)(2,1)S(1)}, u32[]{:S(2)}, u32[]{:S(2)}) collective-permute-start(bf16[2,64,256]{2,1,0:T(8,128)(2,1)S(1)} %bitcast.48), channel_id=1, source_target_pairs={{0,15},{1,0},{2,1},{3,2},{4,3},{5,4},{6,5},{7,6},{8,7},{9,8},{10,9... | collective-permute-start | bytes 196616 | tf_op jit(solution)/shard_map/ppermute | solution.py:74
  21.7 43.2 %copy-start.7 = (bf16[128,256]{1,0:T(8,128)(2,1)S(1)}, bf16[128,256]{1,0:T(8,128)(2,1)}, u32[]{:S(2)}) copy-start(bf16[128,256]{1,0:T(8,128)(2,1)} %copy-done.6) | copy-start | bytes 196612
  23.2 13.4 %copy-start.10 = (bf16[2,64,256]{2,1,0:T(8,128)(2,1)}, bf16[2,64,256]{2,1,0:T(8,128)(2,1)S(1)}, u32[]{:S(2)}) copy-start(bf16[2,64,256]{2,1,0:T(8,128)(2,1)S(1)} %collective-permute-done) | copy-start | bytes 196612
  23.2 6.6 %collective-permute-start.2 = (bf16[2,64,256]{2,1,0:T(8,128)(2,1)S(1)}, bf16[2,64,256]{2,1,0:T(8,128)(2,1)S(1)}, u32[]{:S(2)}, u32[]{:S(2)}) collective-permute-start(bf16[2,64,256]{2,1,0:T(8,128)(2,1)S(1)} %collective-permute-done), channel_id=1, source_target_pairs={{0,1},{1,2},{2,3},{3,4},{4,5},{5,6},{6,7},{7,8},{8,9},{9,10},{10,1... | collective-permute-start | bytes 196616 | tf_op jit(solution)/shard_map/ppermute | solution.py:69
  23.6 41.0 %copy-start.8 = (bf16[2,64,256]{2,1,0:T(8,128)(2,1)}, bf16[2,64,256]{2,1,0:T(8,128)(2,1)S(1)}, u32[]{:S(2)}) copy-start(bf16[2,64,256]{2,1,0:T(8,128)(2,1)S(1)} %collective-permute-done.1) | copy-start | bytes 196612
  23.6 7.4 %collective-permute-start.3 = (bf16[2,64,256]{2,1,0:T(8,128)(2,1)S(1)}, bf16[2,64,256]{2,1,0:T(8,128)(2,1)S(1)}, u32[]{:S(2)}, u32[]{:S(2)}) collective-permute-start(bf16[2,64,256]{2,1,0:T(8,128)(2,1)S(1)} %collective-permute-done.1), channel_id=1, source_target_pairs={{0,15},{1,0},{2,1},{3,2},{4,3},{5,4},{6,5},{7,6},{8,7},{9,8},{10,9... | collective-permute-start | bytes 196616 | tf_op jit(solution)/shard_map/ppermute | solution.py:74
  29.9 6.8 %collective-permute-start.4 = (bf16[2,64,256]{2,1,0:T(8,128)(2,1)S(1)}, bf16[2,64,256]{2,1,0:T(8,128)(2,1)S(1)}, u32[]{:S(2)}, u32[]{:S(2)}) collective-permute-start(bf16[2,64,256]{2,1,0:T(8,128)(2,1)S(1)} %collective-permute-done.2), channel_id=1, source_target_pairs={{0,1},{1,2},{2,3},{3,4},{4,5},{5,6},{6,7},{7,8},{8,9},{9,10},{10,1... | collective-permute-start | bytes 196616 | tf_op jit(solution)/shard_map/ppermute | solution.py:69
  31.0 5.6 %copy-start.11 = (bf16[2,64,256]{2,1,0:T(8,128)(2,1)}, bf16[2,64,256]{2,1,0:T(8,128)(2,1)S(1)}, u32[]{:S(2)}) copy-start(bf16[2,64,256]{2,1,0:T(8,128)(2,1)S(1)} %collective-permute-done.3) | copy-start | bytes 196612
  31.0 6.6 %collective-permute-start.5 = (bf16[2,64,256]{2,1,0:T(8,128)(2,1)S(1)}, bf16[2,64,256]{2,1,0:T(8,128)(2,1)S(1)}, u32[]{:S(2)}, u32[]{:S(2)}) collective-permute-start(bf16[2,64,256]{2,1,0:T(8,128)(2,1)S(1)} %collective-permute-done.3), channel_id=1, source_target_pairs={{0,15},{1,0},{2,1},{3,2},{4,3},{5,4},{6,5},{7,6},{8,7},{9,8},{10,9... | collective-permute-start | bytes 196616 | tf_op jit(solution)/shard_map/ppermute | solution.py:74
  36.7 6.5 %collective-permute-start.6 = (bf16[2,64,256]{2,1,0:T(8,128)(2,1)S(1)}, bf16[2,64,256]{2,1,0:T(8,128)(2,1)S(1)}, u32[]{:S(2)}, u32[]{:S(2)}) collective-permute-start(bf16[2,64,256]{2,1,0:T(8,128)(2,1)S(1)} %collective-permute-done.4), channel_id=1, source_target_pairs={{0,1},{1,2},{2,3},{3,4},{4,5},{5,6},{6,7},{7,8},{8,9},{9,10},{10,1... | collective-permute-start | bytes 196616 | tf_op jit(solution)/shard_map/ppermute | solution.py:69
  37.6 7.4 %collective-permute-start.7 = (bf16[2,64,256]{2,1,0:T(8,128)(2,1)S(1)}, bf16[2,64,256]{2,1,0:T(8,128)(2,1)S(1)}, u32[]{:S(2)}, u32[]{:S(2)}) collective-permute-start(bf16[2,64,256]{2,1,0:T(8,128)(2,1)S(1)} %collective-permute-done.5), channel_id=1, source_target_pairs={{0,15},{1,0},{2,1},{3,2},{4,3},{5,4},{6,5},{7,6},{8,7},{9,8},{10,9... | collective-permute-start | bytes 196616 | tf_op jit(solution)/shard_map/ppermute | solution.py:74
  43.2 7.6 %collective-permute-start.8 = (bf16[2,64,256]{2,1,0:T(8,128)(2,1)S(1)}, bf16[2,64,256]{2,1,0:T(8,128)(2,1)S(1)}, u32[]{:S(2)}, u32[]{:S(2)}) collective-permute-start(bf16[2,64,256]{2,1,0:T(8,128)(2,1)S(1)} %collective-permute-done.6), channel_id=1, source_target_pairs={{0,1},{1,2},{2,3},{3,4},{4,5},{5,6},{6,7},{7,8},{8,9},{9,10},{10,1... | collective-permute-start | bytes 196616 | tf_op jit(solution)/shard_map/ppermute | solution.py:69
  45.0 5.8 %copy-start.15 = (bf16[2,64,256]{2,1,0:T(8,128)(2,1)}, bf16[2,64,256]{2,1,0:T(8,128)(2,1)S(1)}, u32[]{:S(2)}) copy-start(bf16[2,64,256]{2,1,0:T(8,128)(2,1)S(1)} %collective-permute-done.7) | copy-start | bytes 196612
  45.0 6.9 %collective-permute-start.9 = (bf16[2,64,256]{2,1,0:T(8,128)(2,1)S(1)}, bf16[2,64,256]{2,1,0:T(8,128)(2,1)S(1)}, u32[]{:S(2)}, u32[]{:S(2)}) collective-permute-start(bf16[2,64,256]{2,1,0:T(8,128)(2,1)S(1)} %collective-permute-done.7), channel_id=1, source_target_pairs={{0,15},{1,0},{2,1},{3,2},{4,3},{5,4},{6,5},{7,6},{8,7},{9,8},{10,9... | collective-permute-start | bytes 196616 | tf_op jit(solution)/shard_map/ppermute | solution.py:74
  50.8 6.7 %collective-permute-start.10 = (bf16[2,64,256]{2,1,0:T(8,128)(2,1)S(1)}, bf16[2,64,256]{2,1,0:T(8,128)(2,1)S(1)}, u32[]{:S(2)}, u32[]{:S(2)}) collective-permute-start(bf16[2,64,256]{2,1,0:T(8,128)(2,1)S(1)} %collective-permute-done.8), channel_id=1, source_target_pairs={{0,1},{1,2},{2,3},{3,4},{4,5},{5,6},{6,7},{7,8},{8,9},{9,10},{10,1... | collective-permute-start | bytes 196616 | tf_op jit(solution)/shard_map/ppermute | solution.py:69
  51.9 13.0 %copy-start.17 = (bf16[2,64,256]{2,1,0:T(8,128)(2,1)}, bf16[2,64,256]{2,1,0:T(8,128)(2,1)S(1)}, u32[]{:S(2)}) copy-start(bf16[2,64,256]{2,1,0:T(8,128)(2,1)S(1)} %collective-permute-done.9) | copy-start | bytes 196612
  51.9 8.1 %collective-permute-start.11 = (bf16[2,64,256]{2,1,0:T(8,128)(2,1)S(1)}, bf16[2,64,256]{2,1,0:T(8,128)(2,1)}, u32[]{:S(2)}, u32[]{:S(2)}) collective-permute-start(bf16[2,64,256]{2,1,0:T(8,128)(2,1)S(1)} %collective-permute-done.9), channel_id=1, source_target_pairs={{0,15},{1,0},{2,1},{3,2},{4,3},{5,4},{6,5},{7,6},{8,7},{9,8},{10,9... | collective-permute-start | bytes 196616 | tf_op jit(solution)/shard_map/ppermute | solution.py:74
  57.5 7.4 %copy-start.18 = (bf16[2,64,256]{2,1,0:T(8,128)(2,1)}, bf16[2,64,256]{2,1,0:T(8,128)(2,1)S(1)}, u32[]{:S(2)}) copy-start(bf16[2,64,256]{2,1,0:T(8,128)(2,1)S(1)} %collective-permute-done.10) | copy-start | bytes 196612
  57.5 7.1 %collective-permute-start.12 = (bf16[2,64,256]{2,1,0:T(8,128)(2,1)S(1)}, bf16[2,64,256]{2,1,0:T(8,128)(2,1)}, u32[]{:S(2)}, u32[]{:S(2)}) collective-permute-start(bf16[2,64,256]{2,1,0:T(8,128)(2,1)S(1)} %collective-permute-done.10), channel_id=1, source_target_pairs={{0,1},{1,2},{2,3},{3,4},{4,5},{5,6},{6,7},{7,8},{8,9},{9,10},{10,1... | collective-permute-start | bytes 196616 | tf_op jit(solution)/shard_map/ppermute | solution.py:69
  59.9 48.0 %collective-permute-start.13 = (bf16[2,64,256]{2,1,0:T(8,128)(2,1)}, bf16[2,64,256]{2,1,0:T(8,128)(2,1)}, u32[]{:S(2)}, u32[]{:S(2)}) collective-permute-start(bf16[2,64,256]{2,1,0:T(8,128)(2,1)} %collective-permute-done.11), channel_id=1, source_target_pairs={{0,15},{1,0},{2,1},{3,2},{4,3},{5,4},{6,5},{7,6},{8,7},{9,8},{10,9... | collective-permute-start | bytes 196616 | tf_op jit(solution)/shard_map/ppermute | solution.py:74
  64.6 46.7 %collective-permute-start.14 = (bf16[2,64,256]{2,1,0:T(8,128)(2,1)}, bf16[2,64,256]{2,1,0:T(8,128)(2,1)}, u32[]{:S(2)}, u32[]{:S(2)}) collective-permute-start(bf16[2,64,256]{2,1,0:T(8,128)(2,1)} %collective-permute-done.12), channel_id=1, source_target_pairs={{0,1},{1,2},{2,3},{3,4},{4,5},{5,6},{6,7},{7,8},{8,9},{9,10},{10,1... | collective-permute-start | bytes 196616 | tf_op jit(solution)/shard_map/ppermute | solution.py:69
  130.8 38.5 %copy-start.5 = (bf16[2,128,1280]{2,1,0:T(8,128)(2,1)S(1)}, bf16[2,128,1280]{2,1,0:T(8,128)(2,1)}, u32[]{:S(2)}) copy-start(bf16[2,128,1280]{2,1,0:T(8,128)(2,1)} %fusion.13) | copy-start | bytes 1966084
  169.3 7.3 %copy-start.19 = (f32[3,1536]{1,0:T(4,128)S(1)}, f32[3,1536]{1,0:T(4,128)}, u32[]{:S(2)}) copy-start(f32[3,1536]{1,0:T(4,128)} %param.20) | copy-start | bytes 55300
  173.1 3.5 %collective-permute-start.15 = (bf16[2,1,1536]{2,1,0:T(2,128)(2,1)S(1)}, bf16[2,1,1536]{2,1,0:T(2,128)(2,1)S(1)}, u32[]{:S(2)}, u32[]{:S(2)}) collective-permute-start(bf16[2,1,1536]{2,1,0:T(2,128)(2,1)S(1)} %get-tuple-element.8), channel_id=1, source_target_pairs={{0,1},{1,2},{2,3},{3,4},{4,5},{5,6},{6,7},{7,8},{8,9},{9,10},{10,1... | collective-permute-start | bytes 18440 | tf_op jit(solution)/shard_map/ppermute | solution.py:19
  175.2 3.1 %collective-permute-start.16 = (bf16[2,1,1536]{2,1,0:T(2,128)(2,1)S(1)}, bf16[2,1,1536]{2,1,0:T(2,128)(2,1)S(1)}, u32[]{:S(2)}, u32[]{:S(2)}) collective-permute-start(bf16[2,1,1536]{2,1,0:T(2,128)(2,1)S(1)} %get-tuple-element.9), channel_id=1, source_target_pairs={{1,0},{2,1},{3,2},{4,3},{5,4},{6,5},{7,6},{8,7},{9,8},{10,9},{11,1... | collective-permute-start | bytes 18440 | tf_op jit(solution)/shard_map/ppermute | solution.py:21
  (9 other events, 21.8 us)
Sparse Core Ops, SparseCore 0:
  13.4 50.8 all-gather.4
  66.6 52.9 all-gather.6
  121.9 47.3 all-gather.8
  171.4 52.4 all-gather.10
